TPU v7x, 32 devices: a whole 2x2x4 slice. The times are simulated.
32 devices in a mesh: groups: 2 (over y), dp: 4 (over x, core), expert: 4 (over z).
Axes of the slice: x: 2, y: 2, z: 4, core: 2. Of those that a mesh axis runs over, the one named last changes fastest.
Arguments:
- tokens: bfloat16 [2, 64, 7168], P(None, ('groups', 'dp', 'expert')), parts along dimension 1, may hold values from -6 to 6
- expert_ids: int32 [2, 64, 2], P(None, ('groups', 'dp', 'expert')), parts along dimension 1, may hold values from 0 to 3, all different within a row; in each aligned block of 2 rows (0 to 1, 2 to 3, ..., all dimensions but the last counted through in order) at most 2 rows name the same one
- router_weight: bfloat16 [7168, 4], replicated, may hold values from -0.0625 to 0.0625
- w_in: bfloat16 [7168, 2, 8192], P('dp', None, 'expert'), may hold values from -0.0625 to 0.0625
- w_down: bfloat16 [8192, 7168], P('expert', 'dp'), may hold values from -0.125 to 0.125
Outputs:
- combined: bfloat16 [2, 64, 7168], P(None, ('groups', 'dp', 'expert')), parts along dimension 1
There are 2 independent parts, one for each index of `groups`. A program takes and returns all parts, laid end to end along the dimension named above; an argument that names none is the same for every part. Nothing has to cross between parts.
Inputs may be any that keep to these rules, and one draw needn't show every extreme that they name: `expert_ids`: each token names 2 different experts. Within the 2 tokens of one device in one micro-batch (aligned blocks of rows, micro-batch major), no expert is named by more than 2 tokens, a bound that some block reaches.
All inputs are finite; a program needn't handle non-finite values.
Results may differ from a plain program's by a relative error of at most 0.02.
Values may be sent and summed in bfloat16 or wider, within the bound.
A program may use at most 128 MiB of HBM per device.

v0:
```python
import jax
import jax.numpy as jnp
from jax import lax
from jax.sharding import PartitionSpec as P

route_scale = 2.5


def serve_rows(received, w_in, w_down):
    quarter = w_in.shape[0]
    hidden_units = w_down.shape[0]
    w_flat = w_in.reshape(quarter, 2 * hidden_units)
    partial_value = jnp.einsum(
        "mpsrd,df->mpsrf", received, w_flat, preferred_element_type=jnp.float32
    )
    gate_up = lax.psum(partial_value.astype(jnp.bfloat16), "dp").astype(jnp.float32)
    hidden = (jax.nn.silu(gate_up[..., :hidden_units]) * gate_up[..., hidden_units:]).astype(
        jnp.bfloat16
    )
    produced = jnp.einsum("mpsrf,fd->mpsrd", hidden, w_down, preferred_element_type=jnp.float32)
    return produced.astype(jnp.bfloat16)


def body(tokens, expert_ids, router_weight, w_in, w_down):
    num_micro, tok_rows, model_width = tokens.shape
    top_count = expert_ids.shape[2]
    experts = router_weight.shape[1]
    expert_devices = lax.axis_size("expert")
    dp_count = lax.axis_size("dp")
    quarter = model_width // dp_count
    sharers = expert_devices // experts
    capacity = max(2, 2 * tok_rows * top_count // experts)
    logits = jnp.einsum("mtd,de->mte", tokens, router_weight, preferred_element_type=jnp.float32)
    scores = jax.nn.sigmoid(logits)
    chosen = jnp.take_along_axis(scores, expert_ids, axis=2)
    gate_vals = route_scale * chosen / jnp.sum(chosen, axis=2, keepdims=True)
    onehot = (
        expert_ids[..., None] == lax.broadcasted_iota(jnp.int32, (1, 1, 1, experts), 3)
    ).astype(jnp.int32)
    hit_counts = jnp.sum(onehot, axis=2)
    before = jnp.cumsum(hit_counts, axis=1) - hit_counts
    position = jnp.take_along_axis(before, expert_ids, axis=2)
    flat_slots = (expert_ids * capacity + position).reshape(num_micro, tok_rows * top_count)
    token_of = jnp.broadcast_to(
        jnp.arange(tok_rows, dtype=jnp.int32)[:, None], (tok_rows, top_count)
    ).reshape(-1)
    holder = jnp.full((num_micro, experts * capacity), tok_rows, jnp.int32)
    holder = jax.vmap(lambda lookup, places: lookup.at[places].set(token_of))(holder, flat_slots)
    quartered = tokens.reshape(num_micro, tok_rows, dp_count, quarter).transpose(0, 2, 1, 3)
    padded = jnp.concatenate(
        [quartered, jnp.zeros((num_micro, dp_count, 1, quarter), tokens.dtype)], axis=2
    )
    outgoing = jax.vmap(lambda source_rows, row_index: source_rows[:, row_index])(padded, holder)
    outgoing = outgoing.reshape(num_micro, dp_count, experts, 1, capacity, quarter)
    outgoing = jnp.broadcast_to(
        outgoing, (num_micro, dp_count, experts, sharers, capacity, quarter)
    )
    outgoing = outgoing.reshape(num_micro, dp_count, expert_devices, capacity, quarter)
    received = lax.all_to_all(
        lax.all_to_all(outgoing, "dp", split_axis=1, concat_axis=1, tiled=True),
        "expert",
        split_axis=2,
        concat_axis=2,
        tiled=True,
    )
    produced = serve_rows(received, w_in, w_down)
    returned = lax.all_to_all(
        lax.all_to_all(produced, "dp", split_axis=1, concat_axis=1, tiled=True),
        "expert",
        split_axis=2,
        concat_axis=2,
        tiled=True,
    )
    returned = returned.reshape(num_micro, dp_count, experts, sharers, capacity, quarter)
    expert_out = jnp.sum(returned.astype(jnp.float32), axis=3).astype(jnp.bfloat16)
    expert_out = expert_out.reshape(num_micro, dp_count, experts * capacity, quarter)
    picked = jax.vmap(lambda source_rows, row_index: source_rows[:, row_index])(
        expert_out, flat_slots
    )
    picked = picked.reshape(num_micro, dp_count, tok_rows, top_count, quarter)
    summed = jnp.sum(gate_vals[:, None, :, :, None] * picked.astype(jnp.float32), axis=3)
    combined = summed.transpose(0, 2, 1, 3).reshape(num_micro, tok_rows, model_width)
    return combined.astype(jnp.bfloat16)


def solution(mesh):
    placed = (
        P(None, ("groups", "dp", "expert"), None),
        P(None, ("groups", "dp", "expert"), None),
        P(),
        P("dp", None, "expert"),
        P("expert", "dp"),
    )
    return jax.shard_map(
        body,
        mesh=mesh,
        in_specs=placed,
        out_specs=P(None, ("groups", "dp", "expert"), None),
        check_vma=False,
    )
```

profile of v0, /device:TPU:0, one launch (start us, length us, event | category | flops | bytes accessed | tf_op | source)
XLA Modules:
  0.0 131.3 jit_solution(10057357462637629493)
XLA Ops:
  6.5 0.0 copy-start
  6.5 0.8 fusion.19
  7.3 0.7 bitcast_or_fusion
  8.0 0.1 reshape.75
  8.1 0.1 reshape.104
  8.2 0.1 reshape.78
  8.3 0.7 gather_fusion.1
  9.0 0.1 reshape.87
  9.0 0.7 select_add_fusion
  9.8 0.1 reshape.74
  9.8 0.1 reshape.102
  9.9 0.8 scatter_fusion
  10.8 0.1 reshape.90
  10.9 0.9 reshape.73
  11.8 0.8 gather_fusion.2
  12.5 0.1 copy.14
  12.6 9.7 %all_to_all.20 = bf16[2,4,4,2,1792]{4,2,3,0,1:T(4,128)(2,1)S(1)} all-to-all(bf16[2,4,4,2,1792]{4,2,3,0,1:T(4,128)(2,1)S(1)} %copy.14), channel_id=1, replica_groups=mesh['groups'=2,'dp'=4,'expert'=4] {'dp'}, dimensions={1} | all-to-all | bytes 458752 | tf_op jit(solution)/shard_map/all_to_all | solution.py:60
  22.3 0.9 copy.15
  23.2 4.9 %all-to-all-start.1 = ((bf16[2,4,4,2,1792]{4,3,1,0,2:T(2,128)(2,1)}), bf16[2,4,4,2,1792]{4,3,1,0,2:T(2,128)(2,1)S(1)}, u32[]{:S(2)}, u32[]{:S(2)}) async-start(bf16[2,4,4,2,1792]{4,3,1,0,2:T(2,128)(2,1)} %copy.15), calls=%async_computation.1 | async-start | bytes 458752 | tf_op jit(solution)/shard_map/all_to_all | solution.py:59
  28.1 0.0 all-reduce.3.cloned.1.call-start
  28.1 24.3 %reshape.120 = bf16[1792,4096,1,1,1]{1,0,2,3,4:T(8,128)(2,1)} reshape(bf16[1792,2,2048]{2,1,0:T(2,128)(2,1)} %param.8) | data formatting | bytes 29360128 | tf_op jit(solution)/shard_map/reshape | solution.py:12
  52.4 0.0 copy-start.1
  52.4 0.0 all-to-all-done.1
  52.4 9.1 %fusion.4 = bf16[2,4,4,2,4096]{4,2,3,1,0:T(4,128)(2,1)} fusion(bf16[1792,4096,1,1,1]{1,0,2,3,4:T(8,128)(2,1)} %reshape.120, bf16[2,4,4,2,1792]{4,3,1,0,2:T(2,128)(2,1)S(1)} %all-to-all-done.1), kind=kOutput, calls=%fused_computation.9 | convolution fusion | flops 939786240 | bytes 15433728 | tf_op jit(solution)/shard_map/mpsrd,df->mpsrf/dot_general | solution.py:13
  61.5 0.0 all-reduce.3.cloned.1.call-update
  61.5 33.9 %all-reduce.3.cloned.1.call-done = bf16[2,4,4,2,4096]{4,2,3,1,0:T(4,128)(2,1)} async-done(((bf16[2,4,4,2,4096]{4,2,3,1,0:T(4,128)(2,1)}), bf16[2,4,4,2,4096]{4,2,3,1,0:T(4,128)(2,1)}) %all-reduce.3.cloned.1.call-update) | async-done | bytes 524304 | tf_op jit(solution)/shard_map/psum | solution.py:16
  95.4 1.1 convert_element_type.39
  96.6 4.8 %fusion.7 = bf16[2,4,4,2,1792]{4,2,3,1,0:T(4,128)(2,1)S(1)} fusion(bf16[2048,1792]{1,0:T(8,128)(2,1)} %param.9, f32[2,4,4,2,4096]{4,2,3,1,0:T(4,128)S(1)} %convert_element_type.39), kind=kOutput, calls=%fused_computation.10 | convolution fusion | flops 470663168 | bytes 8617984 | tf_op jit(solution)/shard_map/mpsrf,fd->mpsrd/dot_general | solution.py:20
  101.4 0.1 copy.17
  101.5 8.1 %all_to_all.21 = bf16[2,4,4,2,1792]{4,2,3,0,1:T(4,128)(2,1)S(1)} all-to-all(bf16[2,4,4,2,1792]{4,2,3,0,1:T(4,128)(2,1)S(1)} %copy.17), channel_id=1, replica_groups=mesh['groups'=2,'dp'=4,'expert'=4] {'dp'}, dimensions={1} | all-to-all | bytes 458752 | tf_op jit(solution)/shard_map/all_to_all | solution.py:68
  109.6 0.9 copy.18
  110.4 4.6 %all-to-all-start.3 = ((bf16[2,4,4,2,1792]{4,3,1,0,2:T(2,128)(2,1)}), bf16[2,4,4,2,1792]{4,3,1,0,2:T(2,128)(2,1)S(1)}, u32[]{:S(2)}, u32[]{:S(2)}) async-start(bf16[2,4,4,2,1792]{4,3,1,0,2:T(2,128)(2,1)} %copy.18), calls=%async_computation.3 | async-start | bytes 458752 | tf_op jit(solution)/shard_map/all_to_all | solution.py:67
  115.0 0.0 copy-done
  115.0 0.0 copy-done.1
  115.0 0.3 fusion.12
  115.4 0.7 gather_fusion
  116.0 0.1 reshape.81
  116.1 0.1 reshape.96
  116.2 0.1 multiply_divide_fusion
  116.3 6.7 %all-to-all-done.3 = bf16[2,4,4,2,1792]{4,3,1,0,2:T(2,128)(2,1)S(1)} async-done(((bf16[2,4,4,2,1792]{4,3,1,0,2:T(2,128)(2,1)}), bf16[2,4,4,2,1792]{4,3,1,0,2:T(2,128)(2,1)S(1)}, u32[]{:S(2)}, u32[]{:S(2)}) %all-to-all-start.3) | async-done | bytes 229408 | tf_op jit(solution)/shard_map/all_to_all | solution.py:67
  122.9 0.1 copy.19
  123.0 0.7 gather_fusion.3
  123.7 0.1 multiply_reduce_fusion
  123.8 0.6 convert_element_type.47
  (9 shorter events, 0.1 us)
Async XLA Ops:
  6.5 108.5 %copy-start = (bf16[7168,4]{0,1:T(4,128)(2,1)S(1)}, bf16[7168,4]{0,1:T(4,128)(2,1)}, u32[]{:S(2)}) copy-start(bf16[7168,4]{0,1:T(4,128)(2,1)} %param.7) | copy-start | bytes 172036
  23.2 29.2 %all-to-all-start.1 = ((bf16[2,4,4,2,1792]{4,3,1,0,2:T(2,128)(2,1)}), bf16[2,4,4,2,1792]{4,3,1,0,2:T(2,128)(2,1)S(1)}, u32[]{:S(2)}, u32[]{:S(2)}) async-start(bf16[2,4,4,2,1792]{4,3,1,0,2:T(2,128)(2,1)} %copy.15), calls=%async_computation.1 | async-start | bytes 458752 | tf_op jit(solution)/shard_map/all_to_all | solution.py:59
  28.1 67.4 %all-reduce.3.cloned.1.call-start = ((), (), s32[]{:S(2)}) async-start(), calls=%async_computation.4 | async-start | bytes 1048576 | tf_op jit(solution)/shard_map/psum | solution.py:16
  52.4 62.7 %copy-start.1 = (bf16[2,2,7168]{2,1,0:T(2,128)(2,1)S(1)}, bf16[2,2,7168]{2,1,0:T(2,128)(2,1)}, u32[]{:S(2)}) copy-start(bf16[2,2,7168]{2,1,0:T(2,128)(2,1)} %param.5) | copy-start | bytes 172036
  110.4 12.5 %all-to-all-start.3 = ((bf16[2,4,4,2,1792]{4,3,1,0,2:T(2,128)(2,1)}), bf16[2,4,4,2,1792]{4,3,1,0,2:T(2,128)(2,1)S(1)}, u32[]{:S(2)}, u32[]{:S(2)}) async-start(bf16[2,4,4,2,1792]{4,3,1,0,2:T(2,128)(2,1)} %copy.18), calls=%async_computation.3 | async-start | bytes 458752 | tf_op jit(solution)/shard_map/all_to_all | solution.py:67
Sparse Core Ops, SparseCore 0:
  61.7 33.7 all-reduce.2
where the time goes:
time: 132 us; the launch traced here: 131 us
  waiting for transfers between devices  40.6 us (31%)
  local copies, waits for them, and re-layouts  32.2 us (24%)
  blocking collectives  17.8 us (13%)
  matrix products  14.3 us (11%)
  between operations  13.5 us (10%)
  starting transfers between devices  9.47 us (7%)
  other arithmetic  3.59 us (3%)
    psum x1, waiting for transfers between devices, serve_rows(): lax.psum(partial_value.astype(jnp.bfloat16), 'dp').astype(jnp.float32)  33.9 us
    reshape x1, local copies, waits for them, and re-layouts, serve_rows(): w_flat = w_in.reshape(quarter, 2 * hidden_units)  24.3 us
    all_to_all x1, blocking collectives, body(): lax.all_to_all(outgoing, 'dp', split_axis=1, concat_axis=1, tiled=True)  9.69 us
    dot_general x1, matrix products, serve_rows(): jnp.einsum('mpsrd,df->mpsrf', received, w_flat, preferred_element_type=jn...  9.15 us
    all_to_all x1, blocking collectives, body(): lax.all_to_all(produced, 'dp', split_axis=1, concat_axis=1, tiled=True)  8.06 us
    all_to_all x1, waiting for transfers between devices, body(): lax.all_to_all(lax.all_to_all(produced, 'dp', split_axis=1, concat_axis=1...  6.65 us
    all_to_all x1, starting transfers between devices, body(): lax.all_to_all(lax.all_to_all(outgoing, 'dp', split_axis=1, concat_axis=1...  4.87 us
    dot_general x1, matrix products, serve_rows(): jnp.einsum('mpsrf,fd->mpsrd', hidden, w_down, preferred_element_type=jnp....  4.84 us
  transfers between devices with their start and end apart: 3, of which 2 were waited for; matrix products, arithmetic and copies ran while one was open for 19% of the time, Pallas kernels for 0%

commit v1 on v0

v1 whole, which is shorter than its diff:
```python
import functools
import jax
import jax.numpy as jnp
from jax import lax
from jax.experimental import pallas as pl
from jax.experimental.pallas import tpu as pltpu
from jax.sharding import PartitionSpec as P

route_scale = 2.5
f32 = jnp.float32
bf16 = jnp.bfloat16


def loop(count, step):
    if count <= 32:
        for i in range(count):
            step(i)
    else:
        lax.fori_loop(0, count, lambda i, c: (step(i), c)[1], 0)


def kernel(n_dp, n_exp, ids, tok, rw, w_in, w_down, out, stage, xin, lhs, wv, dv, rs_out, rs_in,
           h_all, acc, o_stage, ret, w_sem, d_sem, x_send, x_recv, rs_send, rs_recv, h_send,
           h_recv, o_send, o_recv):
    num_micro, tok_rows, width = tok.shape
    top = ids.shape[2]
    experts = rw.shape[0]
    sharers = n_exp // experts
    quarter = width // n_dp
    per_dev = num_micro * tok_rows
    peers = n_dp * n_exp
    rows = peers * per_dev
    share = rows // n_dp
    chunks, _, cw = wv.shape
    my_d = lax.axis_index("dp")
    my_z = lax.axis_index("expert")
    me = my_d * n_exp + my_z

    def w_copy(c):
        src = w_in.reshape(2 * quarter, chunks * cw)
        return pltpu.make_async_copy(src.at[:, pl.ds(c * cw, cw)], wv.at[c], w_sem.at[c])

    def d_copy(c):
        return pltpu.make_async_copy(w_down.at[pl.ds(c * cw, cw)], dv.at[c], d_sem.at[c])

    barrier = pltpu.get_barrier_semaphore()

    def peer_of(i):
        p = lax.rem(me + 1 + i, peers)
        return p, p // n_exp, lax.rem(p, n_exp)

    def greet(i):
        _, q, z = peer_of(i)
        pl.semaphore_signal(barrier, inc=1, device_id={"dp": q, "expert": z},
                            device_id_type=pl.DeviceIdType.MESH)

    loop(peers - 1, greet)
    for c in range(chunks):
        w_copy(c).start()
    for c in range(chunks):
        d_copy(c).start()
    mine = jnp.concatenate([tok[m].astype(f32) for m in range(num_micro)], axis=0)
    mine16 = mine.astype(bf16)
    for q in range(n_dp):
        stage[q] = mine16[:, q * quarter:(q + 1) * quarter]
    pl.semaphore_wait(barrier, peers - 1)

    def x_send_to(i):
        _, q, z = peer_of(i)
        pltpu.make_async_remote_copy(
            src_ref=stage.at[q], dst_ref=xin.at[me], send_sem=x_send, recv_sem=x_recv,
            device_id={"dp": q, "expert": z}, device_id_type=pl.DeviceIdType.MESH).start()

    loop(peers - 1, x_send_to)
    xin[me] = stage[my_d]
    logits = lax.dot_general(mine16, rw[...], (((1,), (1,)), ((), ())), preferred_element_type=f32)
    scores = 1.0 / (1.0 + jnp.exp(-logits))
    row = lax.broadcasted_iota(jnp.int32, (per_dev, experts), 0)
    col = lax.broadcasted_iota(jnp.int32, (per_dev, experts), 1)
    picked = jnp.zeros((per_dev, experts), f32)
    for m in range(num_micro):
        for t in range(tok_rows):
            for k in range(top):
                hit = (row == m * tok_rows + t) & (col == ids[m, t, k])
                picked = picked + jnp.where(hit, 1.0, 0.0)
    chosen = scores * picked
    gates = route_scale * chosen / jnp.sum(chosen, axis=1, keepdims=True)

    all_but_one = xin.at[pl.ds(0, peers - 1)]
    pltpu.make_async_copy(all_but_one, all_but_one, x_recv).wait()
    r_i = lax.broadcasted_iota(jnp.int32, (128, 256), 0)
    c_i = lax.broadcasted_iota(jnp.int32, (128, 256), 1)
    even = jnp.where(c_i == 2 * r_i, 1.0, 0.0).astype(bf16)
    odd = jnp.where(c_i == 2 * r_i + 1, 1.0, 0.0).astype(bf16)
    block = min(rows, 64)
    group = block // per_dev

    def expand(b):
        x = jnp.concatenate([xin[b * group + k].astype(f32) for k in range(group)], axis=0)
        x = x.astype(bf16)
        for j in range(quarter // 128):
            piece = x[:, j * 128:(j + 1) * 128]
            for s, spread in enumerate((even, odd)):
                lhs[s, pl.ds(b * block, block), pl.ds(j * 256, 256)] = jnp.dot(
                    piece, spread, preferred_element_type=f32).astype(bf16)

    if rows == block:
        expand(0)
    else:
        lax.fori_loop(0, rows // block, lambda b, c: (expand(b), c)[1], 0)

    def up_chunk(c):
        w_copy(c).wait()
        if rows <= 64:
            res = jnp.dot(lhs[...].reshape(2 * rows, 2 * quarter), wv[c],
                          preferred_element_type=f32).astype(bf16)
            rs_out[c] = res.reshape(2, rows, cw)
        else:
            def part(b, carry):
                at = pl.ds(pl.multiple_of(b * block, block), block)
                for s in range(2):
                    rs_out[c, s, at] = jnp.dot(lhs[s, at], wv[c],
                                               preferred_element_type=f32).astype(bf16)
                return carry
            lax.fori_loop(0, rows // block, part, 0)
        for o in range(1, n_dp):
            t = lax.rem(my_d + o, n_dp)
            pltpu.make_async_remote_copy(
                src_ref=rs_out.at[c, :, pl.ds(pl.multiple_of(t * share, share), share)],
                dst_ref=rs_in.at[c, n_dp - 1 - o], send_sem=rs_send, recv_sem=rs_recv.at[c],
                device_id={"dp": t}, device_id_type=pl.DeviceIdType.MESH).start()

    def hidden_chunk(c):
        pltpu.make_async_copy(rs_in.at[c], rs_in.at[c], rs_recv.at[c]).wait()
        at = pl.ds(pl.multiple_of(my_d * share, share), share)
        total = rs_out[c, :, at].astype(f32)
        for o in range(n_dp - 1):
            total = total + rs_in[c, o].astype(f32)
        gate, up = total[0], total[1]
        h_all[c, my_d] = (gate / (1.0 + jnp.exp(-gate)) * up).astype(bf16)
        for o in range(1, n_dp):
            t = lax.rem(my_d + o, n_dp)
            pltpu.make_async_remote_copy(
                src_ref=h_all.at[c, my_d], dst_ref=h_all.at[c, my_d], send_sem=h_send,
                recv_sem=h_recv.at[c], device_id={"dp": t},
                device_id_type=pl.DeviceIdType.MESH).start()

    def down_chunk(c):
        d_copy(c).wait()
        others = h_all.at[c, pl.ds(0, n_dp - 1)]
        pltpu.make_async_copy(others, others, h_recv.at[c]).wait()
        if rows <= 64:
            part = jnp.dot(h_all[c].reshape(rows, cw), dv[c], preferred_element_type=f32)
            acc[...] = part if c == 0 else acc[...] + part
        else:
            per = share // block

            def part(b, carry):
                src = pl.ds(pl.multiple_of(lax.rem(b, per) * block, block), block)
                at = pl.ds(pl.multiple_of(b * block, block), block)
                value = jnp.dot(h_all[c, b // per, src], dv[c], preferred_element_type=f32)
                acc[at] = value if c == 0 else acc[at] + value
                return carry
            lax.fori_loop(0, rows // block, part, 0)

    lag_h, lag_d = 2, 4
    for step in range(chunks + lag_d):
        if step < chunks:
            up_chunk(step)
        if 0 <= step - lag_h < chunks:
            hidden_chunk(step - lag_h)
        if 0 <= step - lag_d < chunks:
            down_chunk(step - lag_d)

    def spread_out(i):
        v = acc[pl.ds(i * 16, 16), :]
        for k in range(16 // per_dev):
            o_stage[i * (16 // per_dev) + k] = v[k * per_dev:(k + 1) * per_dev].astype(bf16)

    loop(rows // 16, spread_out)

    def o_send_to(i):
        p, q, z = peer_of(i)
        pltpu.make_async_remote_copy(
            src_ref=o_stage.at[p], dst_ref=ret.at[me], send_sem=o_send, recv_sem=o_recv,
            device_id={"dp": q, "expert": z}, device_id_type=pl.DeviceIdType.MESH).start()

    loop(peers - 1, o_send_to)
    ret[me] = o_stage[me]
    back = ret.at[pl.ds(0, peers - 1)]
    pltpu.make_async_copy(back, back, o_recv).wait()
    for q in range(n_dp):
        total = jnp.zeros((per_dev, quarter), f32)
        for e in range(experts):
            part = ret[q * n_exp + e * sharers].astype(f32)
            for s in range(1, sharers):
                part = part + ret[q * n_exp + e * sharers + s].astype(f32)
            total = total + gates[:, e:e + 1] * part
        done = total.astype(bf16)
        for m in range(num_micro):
            out[m, :, pl.ds(q * quarter, quarter)] = total[
                m * tok_rows:(m + 1) * tok_rows].astype(bf16)
    pltpu.make_async_copy(all_but_one, all_but_one, x_send).wait()
    pltpu.make_async_copy(rs_in, rs_in, rs_send).wait()
    sent = h_all.at[:, pl.ds(0, n_dp - 1)]
    pltpu.make_async_copy(sent, sent, h_send).wait()
    pltpu.make_async_copy(back, back, o_send).wait()


def body(n_dp, n_exp, tokens, expert_ids, router_weight, w_in, w_down):
    num_micro, tok_rows, width = tokens.shape
    quarter, _, ff = w_in.shape
    per_dev = num_micro * tok_rows
    peers = n_dp * n_exp
    rows = peers * per_dev
    share = rows // n_dp
    cw = min(256, ff)
    chunks = ff // cw
    vmem = pl.BlockSpec(memory_space=pltpu.VMEM)
    dma = pltpu.SemaphoreType.DMA
    return pl.pallas_call(
        functools.partial(kernel, n_dp, n_exp),
        out_shape=jax.ShapeDtypeStruct(tokens.shape, bf16),
        in_specs=[pl.BlockSpec(memory_space=pltpu.SMEM), vmem, vmem,
                  pl.BlockSpec(memory_space=pl.ANY), pl.BlockSpec(memory_space=pl.ANY)],
        out_specs=vmem,
        scratch_shapes=[
            pltpu.VMEM((n_dp, per_dev, quarter), bf16),
            pltpu.VMEM((peers, per_dev, quarter), bf16),
            pltpu.VMEM((2, rows, 2 * quarter), bf16),
            pltpu.VMEM((chunks, 2 * quarter, cw), bf16),
            pltpu.VMEM((chunks, cw, quarter), bf16),
            pltpu.VMEM((chunks, 2, rows, cw), bf16),
            pltpu.VMEM((chunks, n_dp - 1, 2, share, cw), bf16),
            pltpu.VMEM((chunks, n_dp, share, cw), bf16),
            pltpu.VMEM((rows, quarter), f32),
            pltpu.VMEM((peers, per_dev, quarter), bf16),
            pltpu.VMEM((peers, per_dev, quarter), bf16),
            dma((chunks,)), dma((chunks,)), dma, dma, dma, dma((chunks,)), dma, dma((chunks,)),
            dma, dma,
        ],
        compiler_params=pltpu.CompilerParams(
            collective_id=0, has_side_effects=True, vmem_limit_bytes=56 << 20),
    )(expert_ids, tokens, router_weight.T, w_in, w_down)


def solution(mesh):
    rows = P(None, ("groups", "dp", "expert"), None)
    return jax.shard_map(
        functools.partial(body, mesh.shape["dp"], mesh.shape["expert"]),
        mesh=mesh,
        in_specs=(rows, rows, P(), P("dp", None, "expert"), P("expert", "dp")),
        out_specs=rows,
        check_vma=False,
    )
```

time: 132 us -> 38.1 us (0.29)
  waiting for transfers between devices: 40.6 us -> 0 us
  Pallas kernels: 0 us -> 36.4 us
  local copies, waits for them, and re-layouts: 32.2 us -> 1.48 us
  blocking collectives: 17.8 us -> 0 us
  matrix products: 14.3 us -> 0 us
  between operations: 13.5 us -> 0.01 us
  starting transfers between devices: 9.47 us -> 0 us
  other arithmetic: 3.59 us -> 0 us
    pallas_call x0 -> x1, Pallas kernels: none -> 36.4 us  [body(): pl.pallas_call(functools.partial(kernel, n_dp, n_exp), out_shape=jax.Shap...]
    psum x1 -> x0, waiting for transfers between devices: 33.9 us -> none  [serve_rows(): lax.psum(partial_value.astype(jnp.bfloat16), 'dp').astype(jnp.float32)]
    reshape x4 -> x0, local copies, waits for them, and re-layouts: 25.3 us -> none  [the longest x1 24.3 us: serve_rows(): w_flat = w_in.reshape(quarter, 2 * hidden_units)]
    all_to_all x2 -> x0, blocking collectives: 17.8 us -> none  [the longest x1 9.69 us: body(): lax.all_to_all(outgoing, 'dp', split_axis=1, concat_axis=1, tiled=True)]
    dot_general x3 -> x0, matrix products: 14.3 us -> none  [the longest x1 9.15 us: serve_rows(): jnp.einsum('mpsrd,df->mpsrf', received, w_flat, preferred_element_type=jn...]
    all_to_all x2 -> x0, starting transfers between devices: 9.47 us -> none  [the longest x1 4.87 us: body(): lax.all_to_all(lax.all_to_all(outgoing, 'dp', split_axis=1, concat_axis=1...]
    all_to_all x2 -> x0, waiting for transfers between devices: 6.65 us -> none  [the longest x1 6.65 us: body(): lax.all_to_all(lax.all_to_all(produced, 'dp', split_axis=1, concat_axis=1...]
    gather x8 -> x0, local copies, waits for them, and re-layouts: 3.07 us -> none  [the longest x3 1.49 us: body(): source_rows[:, row_index]]
  transfers between devices with their start and end apart: 3 -> 0, of which waited for: 2 -> 0; matrix products, arithmetic and copies ran while one was open for 19% -> 0% of each run, Pallas kernels for 0% -> 0%
where the time goes in v1:
time: 38.1 us; the launch traced here: 37.9 us
  Pallas kernels  36.4 us (96%)
  local copies, waits for them, and re-layouts  1.48 us (4%)
    pallas_call x1, Pallas kernels, body(): pl.pallas_call(functools.partial(kernel, n_dp, n_exp), out_shape=jax.Shap...  36.4 us
    unnamed x1, local copies, waits for them, and re-layouts  1.48 us

profile of v1, /device:TPU:0, one launch (start us, length us, event | category | flops | bytes accessed | tf_op | source)
XLA Modules:
  0.0 37.9 jit_solution(17807753129112642029)
XLA Ops:
  0.0 36.4 %shard_map.55 = bf16[2,2,7168]{2,1,0:T(2,128)(2,1)} custom-call(s32[2,2,2]{2,1,0:T(2,128)} %ids.1, bf16[2,2,7168]{2,1,0:T(2,128)(2,1)} %tok.1, bf16[4,7168]{1,0:T(4,128)(2,1)} %bitcast.1, bf16[1792,2,2048]{2,1,0:T(2,128)(2,1)} %w_in.1, bf16[2048,1792]{1,0:T(8,128)(2,1)} %w_down.1), custom_call_target="tpu_custom_call" | custom-call | tf_op jit(solution)/shard_map/pallas_call | solution.py:221
  36.5 1.5 %copy.7 = bf16[2,2,7168]{2,1,0:T(2,128)(2,1)} copy(bf16[2,2,7168]{2,1,0:T(2,128)(2,1)} %shard_map.55) | data formatting | bytes 114688

commit v2 on v1

--- a/solution.py
+++ b/solution.py
@@ -19,9 +19,9 @@
         lax.fori_loop(0, count, lambda i, c: (step(i), c)[1], 0)
 
 
-def kernel(n_dp, n_exp, ids, tok, rw, w_in, w_down, out, stage, xin, lhs, wv, dv, rs_out, rs_in,
-           h_all, acc, o_stage, ret, w_sem, d_sem, x_send, x_recv, rs_send, rs_recv, h_send,
-           h_recv, o_send, o_recv):
+def kernel(n_dp, n_exp, ids, tok, rw, w_in, w_down, out, stage, xin, lhs, wv, dv, rs_out, r1,
+           x_out, r2, h_all, acc, o_stage, ret, w_sem, d_sem, x_send, x_recv, r1_send, r1_recv,
+           r2_send, r2_recv, hm_send, hm_recv, hx_send, hx_recv, hf_send, hf_recv, o_send, o_recv):
     num_micro, tok_rows, width = tok.shape
     top = ids.shape[2]
     experts = rw.shape[0]
@@ -32,9 +32,12 @@
     rows = peers * per_dev
     share = rows // n_dp
     chunks, _, cw = wv.shape
+    assert n_dp == 4
     my_d = lax.axis_index("dp")
     my_z = lax.axis_index("expert")
     me = my_d * n_exp + my_z
+    lo, hi = lax.rem(my_d, 2), my_d // 2
+    mate, cross, far = 2 * hi + 1 - lo, 2 * (1 - hi) + lo, 2 * (1 - hi) + 1 - lo
 
     def w_copy(c):
         src = w_in.reshape(2 * quarter, chunks * cw)
@@ -109,46 +112,61 @@
     else:
         lax.fori_loop(0, rows // block, lambda b, c: (expand(b), c)[1], 0)
 
+    def send(src, dst, send_sem, recv_sem, t):
+        pltpu.make_async_remote_copy(
+            src_ref=src, dst_ref=dst, send_sem=send_sem, recv_sem=recv_sem,
+            device_id={"dp": t}, device_id_type=pl.DeviceIdType.MESH).start()
+
+    def arrived(ref, sem):
+        pltpu.make_async_copy(ref, ref, sem).wait()
+
     def up_chunk(c):
         w_copy(c).wait()
         if rows <= 64:
             res = jnp.dot(lhs[...].reshape(2 * rows, 2 * quarter), wv[c],
                           preferred_element_type=f32).astype(bf16)
-            rs_out[c] = res.reshape(2, rows, cw)
+            for t in range(n_dp):
+                for s in range(2):
+                    rs_out[c, t % 2, t // 2, s] = res[s * rows + t * share:
+                                                      s * rows + (t + 1) * share]
         else:
+            per = share // block
+
             def part(b, carry):
-                at = pl.ds(pl.multiple_of(b * block, block), block)
+                src = pl.ds(pl.multiple_of(b * block, block), block)
+                at = pl.ds(pl.multiple_of(lax.rem(b, per) * block, block), block)
+                t = b // per
                 for s in range(2):
-                    rs_out[c, s, at] = jnp.dot(lhs[s, at], wv[c],
-                                               preferred_element_type=f32).astype(bf16)
+                    rs_out[c, lax.rem(t, 2), t // 2, s, at] = jnp.dot(
+                        lhs[s, src], wv[c], preferred_element_type=f32).astype(bf16)
                 return carry
             lax.fori_loop(0, rows // block, part, 0)
-        for o in range(1, n_dp):
-            t = lax.rem(my_d + o, n_dp)
-            pltpu.make_async_remote_copy(
-                src_ref=rs_out.at[c, :, pl.ds(pl.multiple_of(t * share, share), share)],
-                dst_ref=rs_in.at[c, n_dp - 1 - o], send_sem=rs_send, recv_sem=rs_recv.at[c],
-                device_id={"dp": t}, device_id_type=pl.DeviceIdType.MESH).start()
+        send(rs_out.at[c, 1 - lo], r1.at[c], r1_send, r1_recv.at[c], mate)
+
+    def pair_chunk(c):
+        arrived(r1.at[c], r1_recv.at[c])
+        x_out[c] = (rs_out[c, lo, 1 - hi].astype(f32) + r1[c, 1 - hi].astype(f32)).astype(bf16)
+        send(x_out.at[c], r2.at[c], r2_send, r2_recv.at[c], cross)
 
     def hidden_chunk(c):
-        pltpu.make_async_copy(rs_in.at[c], rs_in.at[c], rs_recv.at[c]).wait()
-        at = pl.ds(pl.multiple_of(my_d * share, share), share)
-        total = rs_out[c, :, at].astype(f32)
-        for o in range(n_dp - 1):
-            total = total + rs_in[c, o].astype(f32)
+        own = rs_out[c, lo, hi].astype(f32) + r1[c, hi].astype(f32)
+        arrived(r2.at[c], r2_recv.at[c])
+        total = own + r2[c].astype(f32)
         gate, up = total[0], total[1]
         h_all[c, my_d] = (gate / (1.0 + jnp.exp(-gate)) * up).astype(bf16)
-        for o in range(1, n_dp):
-            t = lax.rem(my_d + o, n_dp)
-            pltpu.make_async_remote_copy(
-                src_ref=h_all.at[c, my_d], dst_ref=h_all.at[c, my_d], send_sem=h_send,
-                recv_sem=h_recv.at[c], device_id={"dp": t},
-                device_id_type=pl.DeviceIdType.MESH).start()
+        here = h_all.at[c, my_d]
+        send(here, here, hx_send, hx_recv.at[c], cross)
+        send(here, here, hm_send, hm_recv.at[c], mate)
+
+    def forward_chunk(c):
+        there = h_all.at[c, cross]
+        arrived(there, hx_recv.at[c])
+        send(there, there, hf_send, hf_recv.at[c], mate)
 
     def down_chunk(c):
         d_copy(c).wait()
-        others = h_all.at[c, pl.ds(0, n_dp - 1)]
-        pltpu.make_async_copy(others, others, h_recv.at[c]).wait()
+        arrived(h_all.at[c, mate], hm_recv.at[c])
+        arrived(h_all.at[c, far], hf_recv.at[c])
         if rows <= 64:
             part = jnp.dot(h_all[c].reshape(rows, cw), dv[c], preferred_element_type=f32)
             acc[...] = part if c == 0 else acc[...] + part
@@ -163,14 +181,11 @@
                 return carry
             lax.fori_loop(0, rows // block, part, 0)
 
-    lag_h, lag_d = 2, 4
-    for step in range(chunks + lag_d):
-        if step < chunks:
-            up_chunk(step)
-        if 0 <= step - lag_h < chunks:
-            hidden_chunk(step - lag_h)
-        if 0 <= step - lag_d < chunks:
-            down_chunk(step - lag_d)
+    stages = ((0, up_chunk), (2, pair_chunk), (4, hidden_chunk), (6, forward_chunk), (8, down_chunk))
+    for step in range(chunks + stages[-1][0]):
+        for lag, stage_of in stages:
+            if 0 <= step - lag < chunks:
+                stage_of(step - lag)
 
     def spread_out(i):
         v = acc[pl.ds(i * 16, 16), :]
@@ -196,14 +211,14 @@
             for s in range(1, sharers):
                 part = part + ret[q * n_exp + e * sharers + s].astype(f32)
             total = total + gates[:, e:e + 1] * part
-        done = total.astype(bf16)
         for m in range(num_micro):
             out[m, :, pl.ds(q * quarter, quarter)] = total[
                 m * tok_rows:(m + 1) * tok_rows].astype(bf16)
     pltpu.make_async_copy(all_but_one, all_but_one, x_send).wait()
-    pltpu.make_async_copy(rs_in, rs_in, rs_send).wait()
-    sent = h_all.at[:, pl.ds(0, n_dp - 1)]
-    pltpu.make_async_copy(sent, sent, h_send).wait()
+    arrived(r1, r1_send)
+    arrived(r2, r2_send)
+    for sem in (hm_send, hx_send, hf_send):
+        arrived(h_all.at[:, 0], sem)
     pltpu.make_async_copy(back, back, o_send).wait()
 
 
@@ -230,14 +245,16 @@
             pltpu.VMEM((2, rows, 2 * quarter), bf16),
             pltpu.VMEM((chunks, 2 * quarter, cw), bf16),
             pltpu.VMEM((chunks, cw, quarter), bf16),
-            pltpu.VMEM((chunks, 2, rows, cw), bf16),
-            pltpu.VMEM((chunks, n_dp - 1, 2, share, cw), bf16),
+            pltpu.VMEM((chunks, 2, 2, 2, share, cw), bf16),
+            pltpu.VMEM((chunks, 2, 2, share, cw), bf16),
+            pltpu.VMEM((chunks, 2, share, cw), bf16),
+            pltpu.VMEM((chunks, 2, share, cw), bf16),
             pltpu.VMEM((chunks, n_dp, share, cw), bf16),
             pltpu.VMEM((rows, quarter), f32),
             pltpu.VMEM((peers, per_dev, quarter), bf16),
             pltpu.VMEM((peers, per_dev, quarter), bf16),
             dma((chunks,)), dma((chunks,)), dma, dma, dma, dma((chunks,)), dma, dma((chunks,)),
-            dma, dma,
+            dma, dma((chunks,)), dma, dma((chunks,)), dma, dma((chunks,)), dma, dma,
         ],
         compiler_params=pltpu.CompilerParams(
             collective_id=0, has_side_effects=True, vmem_limit_bytes=56 << 20),

time: 38.1 us -> 38.7 us (1.016)
  Pallas kernels: 36.4 us -> 37 us
    pallas_call x1, Pallas kernels: 36.4 us -> 37 us  [body(): pl.pallas_call(functools.partial(kernel, n_dp, n_exp), out_shape=jax.Shap...]
where the time goes in v2:
time: 38.7 us; the launch traced here: 38.5 us
  Pallas kernels  37 us (96%)
  local copies, waits for them, and re-layouts  1.48 us (4%)
    pallas_call x1, Pallas kernels, body(): pl.pallas_call(functools.partial(kernel, n_dp, n_exp), out_shape=jax.Shap...  37 us
    unnamed x1, local copies, waits for them, and re-layouts  1.48 us

profile of v2, /device:TPU:0, one launch (start us, length us, event | category | flops | bytes accessed | tf_op | source)
XLA Modules:
  0.0 38.5 jit_solution(11777676647054701418)
XLA Ops:
  0.0 37.0 %shard_map.55 = bf16[2,2,7168]{2,1,0:T(2,128)(2,1)} custom-call(s32[2,2,2]{2,1,0:T(2,128)} %ids.1, bf16[2,2,7168]{2,1,0:T(2,128)(2,1)} %tok.1, bf16[4,7168]{1,0:T(4,128)(2,1)} %bitcast.1, bf16[1792,2,2048]{2,1,0:T(2,128)(2,1)} %w_in.1, bf16[2048,1792]{1,0:T(8,128)(2,1)} %w_down.1), custom_call_target="tpu_custom_call" | custom-call | tf_op jit(solution)/shard_map/pallas_call | solution.py:236
  37.0 1.5 %copy.7 = bf16[2,2,7168]{2,1,0:T(2,128)(2,1)} copy(bf16[2,2,7168]{2,1,0:T(2,128)(2,1)} %shard_map.55) | data formatting | bytes 114688

commit v3 on v1

--- a/solution.py
+++ b/solution.py
@@ -163,7 +163,7 @@
                 return carry
             lax.fori_loop(0, rows // block, part, 0)
 
-    lag_h, lag_d = 2, 4
+    lag_h, lag_d = chunks, 2 * chunks
     for step in range(chunks + lag_d):
         if step < chunks:
             up_chunk(step)
@@ -172,20 +172,22 @@
         if 0 <= step - lag_d < chunks:
             down_chunk(step - lag_d)
 
+    per_step = 16 // per_dev
+
     def spread_out(i):
         v = acc[pl.ds(i * 16, 16), :]
-        for k in range(16 // per_dev):
-            o_stage[i * (16 // per_dev) + k] = v[k * per_dev:(k + 1) * per_dev].astype(bf16)
+        for k in range(per_step):
+            p = i * per_step + k
+            o_stage[p] = v[k * per_dev:(k + 1) * per_dev].astype(bf16)
+
+            @pl.when(p != me)
+            def _():
+                pltpu.make_async_remote_copy(
+                    src_ref=o_stage.at[p], dst_ref=ret.at[me], send_sem=o_send, recv_sem=o_recv,
+                    device_id={"dp": p // n_exp, "expert": p % n_exp},
+                    device_id_type=pl.DeviceIdType.MESH).start()
 
     loop(rows // 16, spread_out)
-
-    def o_send_to(i):
-        p, q, z = peer_of(i)
-        pltpu.make_async_remote_copy(
-            src_ref=o_stage.at[p], dst_ref=ret.at[me], send_sem=o_send, recv_sem=o_recv,
-            device_id={"dp": q, "expert": z}, device_id_type=pl.DeviceIdType.MESH).start()
-
-    loop(peers - 1, o_send_to)
     ret[me] = o_stage[me]
     back = ret.at[pl.ds(0, peers - 1)]
     pltpu.make_async_copy(back, back, o_recv).wait()
@@ -196,7 +198,6 @@
             for s in range(1, sharers):
                 part = part + ret[q * n_exp + e * sharers + s].astype(f32)
             total = total + gates[:, e:e + 1] * part
-        done = total.astype(bf16)
         for m in range(num_micro):
             out[m, :, pl.ds(q * quarter, quarter)] = total[
                 m * tok_rows:(m + 1) * tok_rows].astype(bf16)

time: 38.1 us -> 33.4 us (0.88)
  the two profiles are of different devices: /device:TPU:0 before, /device:TPU:3 now
where the time goes in v3:
time: 33.4 us; the launch traced here: 33.2 us
  Pallas kernels  31.7 us (95%)
  local copies, waits for them, and re-layouts  1.48 us (4%)
    pallas_call x1, Pallas kernels, body(): pl.pallas_call(functools.partial(kernel, n_dp, n_exp), out_shape=jax.Shap...  31.7 us
    unnamed x1, local copies, waits for them, and re-layouts  1.48 us

profile of v3, /device:TPU:3, one launch (start us, length us, event | category | flops | bytes accessed | tf_op | source)
XLA Modules:
  0.0 33.2 jit_solution(11622581899523834803)
XLA Ops:
  0.0 31.7 %shard_map.55 = bf16[2,2,7168]{2,1,0:T(2,128)(2,1)} custom-call(s32[2,2,2]{2,1,0:T(2,128)} %ids.1, bf16[2,2,7168]{2,1,0:T(2,128)(2,1)} %tok.1, bf16[4,7168]{1,0:T(4,128)(2,1)} %bitcast.1, bf16[1792,2,2048]{2,1,0:T(2,128)(2,1)} %w_in.1, bf16[2048,1792]{1,0:T(8,128)(2,1)} %w_down.1), custom_call_target="tpu_custom_call" | custom-call | tf_op jit(solution)/shard_map/pallas_call | solution.py:222
  31.7 1.5 %copy.7 = bf16[2,2,7168]{2,1,0:T(2,128)(2,1)} copy(bf16[2,2,7168]{2,1,0:T(2,128)(2,1)} %shard_map.55) | data formatting | bytes 114688

commit v4 on v3

--- a/solution.py
+++ b/solution.py
@@ -123,7 +123,7 @@
                                                preferred_element_type=f32).astype(bf16)
                 return carry
             lax.fori_loop(0, rows // block, part, 0)
-        for o in range(1, n_dp):
+        for o in (*range(2, n_dp), 1):
             t = lax.rem(my_d + o, n_dp)
             pltpu.make_async_remote_copy(
                 src_ref=rs_out.at[c, :, pl.ds(pl.multiple_of(t * share, share), share)],
@@ -138,7 +138,7 @@
             total = total + rs_in[c, o].astype(f32)
         gate, up = total[0], total[1]
         h_all[c, my_d] = (gate / (1.0 + jnp.exp(-gate)) * up).astype(bf16)
-        for o in range(1, n_dp):
+        for o in (*range(2, n_dp), 1):
             t = lax.rem(my_d + o, n_dp)
             pltpu.make_async_remote_copy(
                 src_ref=h_all.at[c, my_d], dst_ref=h_all.at[c, my_d], send_sem=h_send,
@@ -215,7 +215,7 @@
     peers = n_dp * n_exp
     rows = peers * per_dev
     share = rows // n_dp
-    cw = min(256, ff)
+    cw = min(512, ff)
     chunks = ff // cw
     vmem = pl.BlockSpec(memory_space=pltpu.VMEM)
     dma = pltpu.SemaphoreType.DMA

time: 33.4 us -> 33.7 us (level)
  no operation moved by 1% of the time
where the time goes in v4:
time: 33.7 us; the launch traced here: 33.5 us
  Pallas kernels  32 us (95%)
  local copies, waits for them, and re-layouts  1.48 us (4%)
    pallas_call x1, Pallas kernels, body(): pl.pallas_call(functools.partial(kernel, n_dp, n_exp), out_shape=jax.Shap...  32 us
    unnamed x1, local copies, waits for them, and re-layouts  1.48 us

profile of v4, /device:TPU:3, one launch (start us, length us, event | category | flops | bytes accessed | tf_op | source)
XLA Modules:
  0.0 33.5 jit_solution(18263728463123577125)
XLA Ops:
  0.0 32.0 %shard_map.55 = bf16[2,2,7168]{2,1,0:T(2,128)(2,1)} custom-call(s32[2,2,2]{2,1,0:T(2,128)} %ids.1, bf16[2,2,7168]{2,1,0:T(2,128)(2,1)} %tok.1, bf16[4,7168]{1,0:T(4,128)(2,1)} %bitcast.1, bf16[1792,2,2048]{2,1,0:T(2,128)(2,1)} %w_in.1, bf16[2048,1792]{1,0:T(8,128)(2,1)} %w_down.1), custom_call_target="tpu_custom_call" | custom-call | tf_op jit(solution)/shard_map/pallas_call | solution.py:222
  32.0 1.5 %copy.7 = bf16[2,2,7168]{2,1,0:T(2,128)(2,1)} copy(bf16[2,2,7168]{2,1,0:T(2,128)(2,1)} %shard_map.55) | data formatting | bytes 114688
